TPU v7x, 32 devices: a whole 2x2x4 slice. The times are simulated.
32 devices in a mesh: groups: 2 (over y), mz: 4 (over z), pix: 4 (over x, core).
Axes of the slice: x: 2, y: 2, z: 4, core: 2. Of those that a mesh axis runs over, the one named last changes fastest.
Arguments:
- spectra: bfloat16 [1024, 262144], P(('groups', 'pix'), 'mz'), parts along dimension 0
- kernel: bfloat16 [129], replicated, may hold values from 0.0009994507 to 0.029907227
- probes: bfloat16 [262144, 128], P('mz'), may hold values from -0.01171875 to 0.01171875
Outputs:
- basis: bfloat16 [1024, 128], P(('groups', 'pix')), parts along dimension 0
- projected: bfloat16 [256, 262144], P(('groups', 'pix'), 'mz'), parts along dimension 0
There are 2 independent parts, one for each index of `groups`. A program takes and returns all parts, laid end to end along the dimension named above; an argument that names none is the same for every part. Nothing has to cross between parts.
All inputs are finite; a program needn't handle non-finite values.
Results may differ from a plain program's by a relative error of at most 0.019.
Values may be sent and summed in bfloat16 or wider, within the bound.
A program may use at most 192 MiB of HBM per device.

v0:
```python
import functools
import math

import jax
import jax.numpy as jnp
from jax import lax
from jax.experimental import pallas as pl
from jax.experimental.pallas import tpu as pltpu
from jax.sharding import PartitionSpec as P

LANES = 128
OUT = 256
WIN = OUT + 2 * LANES


def clean_kernel(steps, main, left, right, halo_l, halo_r, u_ref, probes, cleaned, sketch, w_ref):
    step = pl.program_id(0)
    tile = main.shape[1]

    @pl.when(step == 0)
    def _():
        base = jnp.broadcast_to(u_ref[...], (WIN, WIN))
        w_ref[...] = pltpu.roll(base, 0, 1, stride=1, stride_axis=0)[:, :OUT].astype(jnp.bfloat16)
        sketch[...] = jnp.zeros_like(sketch)

    low = jnp.where(step == 0, halo_l[...], left[...])
    high = jnp.where(step == steps - 1, halo_r[...], right[...])
    w = w_ref[...]
    count = tile // OUT
    for j in range(count):
        pieces = []
        begin, end = j * OUT - LANES, (j + 1) * OUT + LANES
        if begin < 0:
            pieces.append(low)
        pieces.append(main[:, max(begin, 0) : min(end, tile)])
        if end > tile:
            pieces.append(high)
        window = pieces[0] if len(pieces) == 1 else jnp.concatenate(pieces, axis=1)
        base = jnp.dot(window, w, preferred_element_type=jnp.float32)
        mine = main[:, j * OUT : (j + 1) * OUT].astype(jnp.float32)
        cleaned[:, j * OUT : (j + 1) * OUT] = (mine - base).astype(jnp.bfloat16)
    sketch[...] += jnp.dot(cleaned[...], probes[...], preferred_element_type=jnp.float32)


def clean_and_sketch(spectra, halo_l, halo_r, u, probes):
    rows, bins = spectra.shape
    cols = probes.shape[1]
    tile = min(4096, bins)
    steps = bins // tile
    per = tile // LANES
    last = bins // LANES - 1
    return pl.pallas_call(
        functools.partial(clean_kernel, steps),
        grid=(steps,),
        in_specs=[
            pl.BlockSpec((rows, tile), lambda i: (0, i)),
            pl.BlockSpec((rows, LANES), lambda i: (0, jnp.maximum(i * per - 1, 0))),
            pl.BlockSpec((rows, LANES), lambda i: (0, jnp.minimum((i + 1) * per, last))),
            pl.BlockSpec((rows, LANES), lambda i: (0, 0)),
            pl.BlockSpec((rows, LANES), lambda i: (0, 0)),
            pl.BlockSpec((1, WIN), lambda i: (0, 0)),
            pl.BlockSpec((tile, cols), lambda i: (i, 0)),
        ],
        out_specs=[
            pl.BlockSpec((rows, tile), lambda i: (0, i)),
            pl.BlockSpec((rows, cols), lambda i: (0, 0)),
        ],
        out_shape=[
            jax.ShapeDtypeStruct((rows, bins), jnp.bfloat16),
            jax.ShapeDtypeStruct((rows, cols), jnp.float32),
        ],
        scratch_shapes=[pltpu.VMEM((WIN, OUT), jnp.bfloat16)],
        compiler_params=pltpu.CompilerParams(
            dimension_semantics=("arbitrary",), vmem_limit_bytes=32 * 2**20
        ),
        cost_estimate=pl.CostEstimate(
            flops=2 * rows * bins * (WIN + cols),
            bytes_accessed=bins * (4 * rows + 2 * cols),
            transcendentals=0,
        ),
    )(spectra, spectra, spectra, halo_l, halo_r, u, probes)


def project_kernel(
    n_pix, factor, basis_t, cleaned, out,
    rows_in, lhs, give, core_in, hold, x_give, x_in, acc, out_v,
    load_sem, give_sem, core_sem, x_send_sem, x_recv_sem, store_sem,
):
    chips = n_pix // 2
    share = basis_t.shape[1]
    half = chips * share
    chunks, width = acc.shape[0], acc.shape[2]
    ring = give.shape[0]
    groups, mz, pix = lax.axis_index("groups"), lax.axis_index("mz"), lax.axis_index("pix")
    core = lax.rem(pix, 2)
    chip = lax.div(pix, 2)
    other = 1 - core

    def device(at_chip, at_core):
        return (groups, mz, at_chip * 2 + at_core)

    def chip_of(d):
        return lax.rem(chip + d, chips)

    def load(k):
        return pltpu.make_async_copy(
            cleaned.at[:, pl.ds(pl.multiple_of(k * width, width), width)],
            rows_in.at[k], load_sem.at[k],
        )

    @pl.loop(0, chunks)
    def _(k):
        load(k).start()

    barrier = pltpu.get_barrier_semaphore()
    pl.semaphore_signal(barrier, inc=1, device_id=device(chip, other), device_id_type=pl.DeviceIdType.MESH)
    for d in range(1, chips):
        pl.semaphore_signal(
            barrier, inc=1, device_id=device(chip_of(d), core), device_id_type=pl.DeviceIdType.MESH
        )

    for d in range(chips):
        lhs[pl.ds(d * share, share), :] = basis_t[chip_of(d) * 2 + other]
        lhs[pl.ds(half + d * share, share), :] = basis_t[chip_of(d) * 2 + core]

    pl.semaphore_wait(barrier, chips)

    def to_core(k):
        return pltpu.make_async_remote_copy(
            src_ref=give.at[lax.rem(k, ring)], dst_ref=core_in.at[k],
            send_sem=give_sem.at[lax.rem(k, ring)], recv_sem=core_sem.at[k],
            device_id=device(chip, other), device_id_type=pl.DeviceIdType.MESH,
        )

    def to_chip(d, k):
        return pltpu.make_async_remote_copy(
            src_ref=x_give.at[d - 1, k], dst_ref=x_in.at[d - 1, k],
            send_sem=x_send_sem.at[d - 1, k], recv_sem=x_recv_sem.at[d - 1, k],
            device_id=device(chip_of(d), core), device_id_type=pl.DeviceIdType.MESH,
        )

    def first(k):
        load(k).wait()
        slot = lax.rem(k, ring)

        @pl.when(k >= ring)
        def _():
            to_core(k - ring).wait_send()

        part = jnp.dot(lhs[...], rows_in[k], preferred_element_type=jnp.float32) * factor
        part = part.astype(jnp.bfloat16)
        give[slot] = part[:half]
        to_core(k).start()
        hold[slot] = part[half:]

    def second(k):
        to_core(k).wait_recv()
        slot = lax.rem(k, ring)
        total = hold[slot].astype(jnp.float32) + core_in[k].astype(jnp.float32)
        acc[k] = total[:share]
        for d in range(1, chips):
            x_give[d - 1, k] = total[d * share : (d + 1) * share].astype(jnp.bfloat16)
            to_chip(d, k).start()

    def store(k):
        return pltpu.make_async_copy(
            out_v.at[k], out.at[:, pl.ds(pl.multiple_of(k * width, width), width)], store_sem.at[k]
        )

    lag = min(ring - 1, chunks)

    @pl.loop(0, lag)
    def _(k):
        first(k)

    @pl.loop(lag, chunks)
    def _(k):
        first(k)
        second(k - lag)

    @pl.loop(chunks - lag, chunks)
    def _(k):
        second(k)

    @pl.loop(max(chunks - ring, 0), chunks)
    def _(k):
        to_core(k).wait_send()

    @pl.loop(0, chunks)
    def _(k):
        total = acc[k]
        for d in range(1, chips):
            to_chip(d, k).wait()
            total = total + x_in[d - 1, k].astype(jnp.float32)
        out_v[k] = total.astype(jnp.bfloat16)
        store(k).start()

    @pl.loop(0, chunks)
    def _(k):
        store(k).wait()


def project(basis, cleaned, n_pix, factor):
    rows, bins = cleaned.shape
    cols = basis.shape[1]
    share = cols // n_pix
    chips = n_pix // 2
    half = chips * share
    width = min(2048, bins)
    chunks = bins // width
    ring = 4
    bf16, f32 = jnp.bfloat16, jnp.float32
    basis_t = basis.T.reshape(n_pix, share, rows)
    away = max(chips - 1, 1)
    return pl.pallas_call(
        functools.partial(project_kernel, n_pix, factor),
        in_specs=[pl.BlockSpec(memory_space=pltpu.VMEM), pl.BlockSpec(memory_space=pl.ANY)],
        out_specs=pl.BlockSpec(memory_space=pl.ANY),
        out_shape=jax.ShapeDtypeStruct((share, bins), bf16),
        scratch_shapes=[
            pltpu.VMEM((chunks, rows, width), bf16),
            pltpu.VMEM((cols, rows), bf16),
            pltpu.VMEM((ring, half, width), bf16),
            pltpu.VMEM((chunks, half, width), bf16),
            pltpu.VMEM((ring, half, width), bf16),
            pltpu.VMEM((away, chunks, share, width), bf16),
            pltpu.VMEM((away, chunks, share, width), bf16),
            pltpu.VMEM((chunks, share, width), f32),
            pltpu.VMEM((chunks, share, width), bf16),
            pltpu.SemaphoreType.DMA((chunks,)),
            pltpu.SemaphoreType.DMA((ring,)),
            pltpu.SemaphoreType.DMA((chunks,)),
            pltpu.SemaphoreType.DMA((away, chunks)),
            pltpu.SemaphoreType.DMA((away, chunks)),
            pltpu.SemaphoreType.DMA((chunks,)),
        ],
        compiler_params=pltpu.CompilerParams(
            collective_id=0, has_side_effects=True, vmem_limit_bytes=56 * 2**20
        ),
        cost_estimate=pl.CostEstimate(
            flops=2 * rows * bins * cols,
            bytes_accessed=2 * bins * (rows + share),
            transcendentals=0,
        ),
    )(basis_t, cleaned)


def per_device(spectra, kernel, probes):
    pix_rows, bin_cols = spectra.shape
    n_pix, n_mz = lax.axis_size("pix"), lax.axis_size("mz")
    all_pixels = pix_rows * n_pix
    factor = 1.0 / math.sqrt(float(all_pixels))
    up = [(i, i + 1) for i in range(n_mz - 1)]
    down = [(b, a) for a, b in up]
    halo_l = lax.ppermute(spectra[:, bin_cols - LANES :], "mz", up)
    halo_r = lax.ppermute(spectra[:, :LANES], "mz", down)
    taps = kernel.shape[0]
    low = WIN - (LANES - taps // 2) - (taps - 1)
    u = jnp.pad(kernel[::-1].astype(jnp.float32), (low, WIN - low - taps))[None, :]
    cleaned, partial_sketch = clean_and_sketch(spectra, halo_l, halo_r, u, probes)
    inner_dims = (((0,), (0,)), ((), ()))
    sketch = lax.psum(partial_sketch, "mz")
    local_gram = lax.dot_general(sketch, sketch, inner_dims, precision=lax.Precision.HIGHEST)
    gram = lax.psum(local_gram, "pix") / float(all_pixels)
    lower = jnp.linalg.cholesky(gram)
    basis = lax.linalg.triangular_solve(
        lower, sketch, left_side=False, lower=True, transpose_a=True
    ).astype(jnp.bfloat16)
    projected = project(basis, cleaned, n_pix, factor)
    return (basis, projected)


def solution(mesh):
    in_specs = (P(("groups", "pix"), "mz"), P(), P("mz", None))
    out_specs = (P(("groups", "pix"), None), P(("groups", "pix"), "mz"))
    return jax.shard_map(
        per_device, mesh=mesh, in_specs=in_specs, out_specs=out_specs, check_vma=False
    )
```

profile of v0, /device:TPU:0, one launch (start us, length us, event | category | flops | bytes accessed | tf_op | source)
XLA Modules:
  0.0 251.6 jit_solution(2973842363612408168)
XLA Ops:
  7.2 0.8 fusion.3
  8.0 1.3 collective-permute-start.1
  9.3 5.6 %collective-permute-start = (bf16[128,128]{1,0:T(8,128)(2,1)S(1)}, bf16[128,128]{1,0:T(8,128)(2,1)S(1)}, u32[]{:S(2)}, u32[]{:S(2)}) collective-permute-start(bf16[128,128]{1,0:T(8,128)(2,1)S(1)} %get-tuple-element.9), channel_id=1, source_target_pairs={{0,4},{4,8},{8,12},{1,5},{5,9},{9,13},{2,6},{6,10},{10,14},{3,7},{... | collective-permute-start | bytes 98312 | tf_op jit(solution)/shard_map/ppermute | solution.py:255
  14.8 0.7 reverse
  15.6 0.1 slice.18
  15.7 0.1 pad_convert_fusion
  15.8 0.7 collective-permute-done.halo_l
  16.4 23.5 %shard_map.50 = (bf16[128,65536]{1,0:T(8,128)(2,1)S(1)}, f32[128,128]{1,0:T(8,128)}) custom-call(bf16[128,65536]{1,0:T(8,128)(2,1)} %right.1, bf16[128,65536]{1,0:T(8,128)(2,1)} %right.1, bf16[128,65536]{1,0:T(8,128)(2,1)} %right.1, bf16[128,128]{1,0:T(8,128)(2,1)S(1)} %collective-permute-done.halo_l, bf16[128,128]{1,0:T(8,128)(2,1)S(1)} %collective-permute-done.1.halo_r, ...), custom_call_target="tpu_custom_call" | custom-call | flops 10737418240 | bytes 50331648 | tf_op jit(solution)/shard_map/pallas_call | solution.py:52
  40.0 5.7 %copy-done = bf16[128,65536]{1,0:T(8,128)(2,1)} copy-done((bf16[128,65536]{1,0:T(8,128)(2,1)}, bf16[128,65536]{1,0:T(8,128)(2,1)S(1)}, u32[]{:S(2)}) %copy-start) | copy-done | bytes 16777240
  45.7 0.0 all-reduce.6.cloned.1.call-start
  45.8 36.5 %all-reduce.4.cloned.1.call-done = f32[128,128]{1,0:T(8,128)} async-done(((f32[128,128]{1,0:T(8,128)}), f32[128,128]{1,0:T(8,128)}) %all-reduce.4.cloned.1.call-update) | async-done | bytes 65552 | tf_op jit(solution)/shard_map/psum | solution.py:262
  82.3 1.8 fusion.4
  84.1 31.9 %all-reduce.6.cloned.1.call-done = f32[128,128]{0,1:T(8,128)} async-done(((f32[128,128]{0,1:T(8,128)}), f32[128,128]{0,1:T(8,128)}) %all-reduce.6.cloned.1.call-update) | async-done | bytes 65552 | tf_op jit(solution)/shard_map/psum | solution.py:264
  116.1 0.8 broadcast_multiply_fusion
  116.9 0.1 copy.6
  117.0 0.9 fusion.2
  117.9 11.7 %cholesky.16 = f32[128,128]{1,0:T(8,128)S(1)} custom-call(f32[128,128]{1,0:T(8,128)S(1)} %fusion.2), custom_call_target="Cholesky" | custom-call | tf_op jit(solution)/shard_map/jit(cholesky)/cholesky | solution.py:265
  129.6 0.6 compare_reduce_fusion
  130.3 0.7 fusion
  130.9 9.8 %custom-call.6 = f32[1,128,128]{1,2,0:T(8,128)S(1)} custom-call(f32[1,128,128]{2,1,0:T(8,128)S(1)} %fusion), custom_call_target="InvertDiagBlocksLowerTriangular" | custom-call | tf_op jit(solution)/shard_map/triangular_solve | solution.py:266
  140.7 1.1 convolution_convert_fusion
  141.9 0.7 copy.7
  142.6 97.7 %shard_map.51 = bf16[32,65536]{1,0:T(8,128)(2,1)} custom-call(bf16[4,32,128]{2,1,0:T(8,128)(2,1)} %bitcast.18, bf16[128,65536]{1,0:T(8,128)(2,1)} %copy-done), custom_call_target="tpu_custom_call" | custom-call | flops 2147483648 | bytes 20971520 | tf_op jit(solution)/shard_map/pallas_call | solution.py:215
  240.3 4.5 %copy.12 = bf16[32,65536]{1,0:T(8,128)(2,1)} copy(bf16[32,65536]{1,0:T(8,128)(2,1)} %shard_map.51) | data formatting | bytes 8388608
  (8 shorter events, 0.1 us)
Async XLA Ops:
  7.2 75.1 %all-reduce.4.cloned.1.call-start = ((), (), s32[]{:S(2)}) async-start(), calls=%async_computation | async-start | bytes 131072 | tf_op jit(solution)/shard_map/psum | solution.py:262
  8.0 7.8 %collective-permute-start.1 = (bf16[128,128]{1,0:T(8,128)(2,1)S(1)}, bf16[128,128]{1,0:T(8,128)(2,1)S(1)}, u32[]{:S(2)}, u32[]{:S(2)}) collective-permute-start(bf16[128,128]{1,0:T(8,128)(2,1)S(1)} %get-tuple-element.8), channel_id=1, source_target_pairs={{4,0},{8,4},{12,8},{5,1},{9,5},{13,9},{6,2},{10,6},{14,10},{7,3},{... | collective-permute-start | bytes 98312 | tf_op jit(solution)/shard_map/ppermute | solution.py:256
  9.3 7.1 %collective-permute-start = (bf16[128,128]{1,0:T(8,128)(2,1)S(1)}, bf16[128,128]{1,0:T(8,128)(2,1)S(1)}, u32[]{:S(2)}, u32[]{:S(2)}) collective-permute-start(bf16[128,128]{1,0:T(8,128)(2,1)S(1)} %get-tuple-element.9), channel_id=1, source_target_pairs={{0,4},{4,8},{8,12},{1,5},{5,9},{9,13},{2,6},{6,10},{10,14},{3,7},{... | collective-permute-start | bytes 98312 | tf_op jit(solution)/shard_map/ppermute | solution.py:255
  40.0 5.7 %copy-start = (bf16[128,65536]{1,0:T(8,128)(2,1)}, bf16[128,65536]{1,0:T(8,128)(2,1)S(1)}, u32[]{:S(2)}) copy-start(bf16[128,65536]{1,0:T(8,128)(2,1)S(1)} %get-tuple-element.5.cleaned) | copy-start | bytes 50331652
  45.7 70.4 %all-reduce.6.cloned.1.call-start = ((), (), s32[]{:S(2)}) async-start(), calls=%async_computation.1 | async-start | bytes 131072 | tf_op jit(solution)/shard_map/psum | solution.py:264
  141.9 0.7 copy-start.1
Sparse Core Ops, SparseCore 0:
  45.8 36.4 all-reduce.3
  85.3 30.7 all-reduce.5
where the time goes:
time: 252 us
  Pallas kernels  121 us (48%)
  waiting for transfers between devices  69.2 us (27%)
  other arithmetic  24.6 us (10%)
  between operations  14.1 us (6%)
  local copies, waits for them, and re-layouts  12.6 us (5%)
  starting transfers between devices  6.92 us (3%)
  matrix products  2.96 us (1%)
    pallas_call x1, Pallas kernels, project(): pl.pallas_call(functools.partial(project_kernel, n_pix, factor), in_specs...  97.7 us
    psum x1, waiting for transfers between devices, per_device(): sketch = lax.psum(partial_sketch, 'mz')  36.5 us
    psum x1, waiting for transfers between devices, per_device(): gram = lax.psum(local_gram, 'pix') / float(all_pixels)  31.9 us
    pallas_call x1, Pallas kernels, clean_and_sketch(): pl.pallas_call(functools.partial(clean_kernel, steps), grid=(steps,), in_...  23.5 us
    another operation x3, other arithmetic, per_device(): lower = jnp.linalg.cholesky(gram)  12.4 us
    unnamed x8, local copies, waits for them, and re-layouts  11.7 us
    another operation x2, other arithmetic, per_device(): lax.linalg.triangular_solve(lower, sketch, left_side=False, lower=True, t...  10.5 us
    ppermute x1, starting transfers between devices, per_device(): halo_l = lax.ppermute(spectra[:, bin_cols - LANES:], 'mz', up)  5.56 us
  transfers between devices with their start and end apart: 4, of which 3 were waited for; matrix products, arithmetic and copies ran while one was open for 0% of the time, Pallas kernels for 0%

commit v1 on v0

v1 whole, which is shorter than its diff:
```python
import functools
import math

import jax
import jax.numpy as jnp
from jax import lax
from jax.experimental import pallas as pl
from jax.experimental.pallas import tpu as pltpu
from jax.sharding import PartitionSpec as P

LANES = 128
OUT = 256
WIN = OUT + 2 * LANES


MESH = pl.DeviceIdType.MESH
HIGHEST = lax.Precision.HIGHEST
PANEL = 8


def whiten(a_ref, x_ref):
    size = a_ref.shape[0]
    row = lax.broadcasted_iota(jnp.int32, (PANEL, 1), 0)
    x_ref[...] = (
        lax.broadcasted_iota(jnp.int32, (size, size), 0)
        == lax.broadcasted_iota(jnp.int32, (size, size), 1)
    ).astype(jnp.float32)

    def panel(index, carry):
        a, x = carry
        p, q = a[:PANEL], x[:PANEL]
        rows_p, rows_q = [], []
        for t in range(PANEL):
            inv = lax.rsqrt(p[t : t + 1, t : t + 1])
            r, y = p[t : t + 1] * inv, q[t : t + 1] * inv
            rows_p.append(r)
            rows_q.append(y)
            if t + 1 < PANEL:
                scale = jnp.where(row > t, p[:, t : t + 1] * inv, 0.0)
                p = p - scale * r
                q = q - scale * y
        r, y = jnp.concatenate(rows_p, axis=0), jnp.concatenate(rows_q, axis=0)
        x_ref[pl.ds(pl.multiple_of(index * PANEL, PANEL), PANEL), :] = y
        turned = r.T
        rest_a, rest_x = a[PANEL:], x[PANEL:]
        for t in range(PANEL):
            scale = turned[PANEL:, t : t + 1]
            rest_a = rest_a - scale * r[t : t + 1]
            rest_x = rest_x - scale * y[t : t + 1]
        zeros = jnp.zeros((PANEL, size), jnp.float32)
        rest_a = pltpu.roll(rest_a, size - PANEL, 1)
        return jnp.concatenate([rest_a, zeros], axis=0), jnp.concatenate([rest_x, zeros], axis=0)

    lax.fori_loop(0, size // PANEL, panel, (a_ref[...], x_ref[...]))


def fused_kernel(
    n_mz, n_pix, factor, pixels, spectra, u_ref, probes, basis, out,
    raw, tap, w_ref, halo, cleaned, total, parts, parts_in, sketch, gram, gram_in, x_ref,
    lhs, give, core_in, hold, x_give, x_in, acc, out_v,
    raw_sem, tap_sem, halo_send, halo_recv, parts_send, parts_recv, all_send, all_recv,
    gram_send, gram_recv, give_sem, core_sem, x_send_sem, x_recv_sem, store_sem,
):
    bins = spectra.shape[1]
    slots, tile = tap.shape[0], tap.shape[1]
    tiles = bins // tile
    chips = n_pix // 2
    share = lhs.shape[0] // n_pix
    half = chips * share
    chunks, width = acc.shape[0], acc.shape[2]
    per = tile // width
    ring = give.shape[0]
    groups, mz, pix = lax.axis_index("groups"), lax.axis_index("mz"), lax.axis_index("pix")
    core = lax.rem(pix, 2)
    chip = lax.div(pix, 2)
    other = 1 - core

    def at_z(d):
        return (groups, lax.rem(mz + d, n_mz), pix)

    def at_pix(d):
        return (groups, mz, lax.rem(pix + d, n_pix))

    def device(at_chip, at_core):
        return (groups, mz, at_chip * 2 + at_core)

    def chip_of(d):
        return lax.rem(chip + d, chips)

    def tile_of(pos):
        return jnp.where(pos == tiles - 1, tiles - 1, jnp.where(pos == tiles - 2, 0, pos + 1))

    def each_load(pos, act):
        slot = lax.rem(pos, slots)

        @pl.when(pos < tiles - 2)
        def _():
            begin = pl.multiple_of((pos + 1) * tile - LANES, LANES)
            act(pltpu.make_async_copy(
                spectra.at[:, pl.ds(begin, tile + 2 * LANES)], raw.at[slot], raw_sem.at[slot]))

        @pl.when(pos == tiles - 2)
        def _():
            act(pltpu.make_async_copy(
                spectra.at[:, pl.ds(0, tile + LANES)],
                raw.at[slot, :, pl.ds(LANES, tile + LANES)], raw_sem.at[slot]))

        @pl.when(pos == tiles - 1)
        def _():
            act(pltpu.make_async_copy(
                spectra.at[:, pl.ds(bins - tile - LANES, tile + LANES)],
                raw.at[slot, :, pl.ds(0, tile + LANES)], raw_sem.at[slot]))

        begin = pl.multiple_of(tile_of(pos) * tile, tile)
        act(pltpu.make_async_copy(probes.at[pl.ds(begin, tile), :], tap.at[slot], tap_sem.at[slot]))

    for pos in range(min(slots, tiles)):
        each_load(jnp.int32(pos), lambda c: c.start())

    barrier = pltpu.get_barrier_semaphore()
    for d in range(1, n_mz):
        pl.semaphore_signal(barrier, inc=1, device_id=at_z(d), device_id_type=MESH)
    for d in range(1, n_pix):
        pl.semaphore_signal(barrier, inc=1, device_id=at_pix(d), device_id_type=MESH)

    base = jnp.broadcast_to(u_ref[...], (WIN, WIN))
    w_ref[...] = pltpu.roll(base, 0, 1, stride=1, stride_axis=0)[:, :OUT].astype(jnp.bfloat16)
    total[...] = jnp.zeros_like(total)

    pl.semaphore_wait(barrier, n_mz - 1 + n_pix - 1)

    to_right = pltpu.make_async_remote_copy(
        src_ref=spectra.at[:, pl.ds(bins - LANES, LANES)], dst_ref=halo.at[0],
        send_sem=halo_send.at[0], recv_sem=halo_recv.at[0],
        device_id=at_z(1), device_id_type=MESH,
    )
    to_left = pltpu.make_async_remote_copy(
        src_ref=spectra.at[:, pl.ds(0, LANES)], dst_ref=halo.at[1],
        send_sem=halo_send.at[1], recv_sem=halo_recv.at[1],
        device_id=at_z(n_mz - 1), device_id_type=MESH,
    )

    @pl.when(mz < n_mz - 1)
    def _():
        to_right.start()

    @pl.when(mz > 0)
    def _():
        to_left.start()

    @pl.when(mz == 0)
    def _():
        halo[0] = jnp.zeros(halo.shape[1:], halo.dtype)

    @pl.when(mz == n_mz - 1)
    def _():
        halo[1] = jnp.zeros(halo.shape[1:], halo.dtype)

    def clean(pos):
        slot = lax.rem(pos, slots)
        at = tile_of(pos)
        each_load(pos, lambda c: c.wait())

        @pl.when(pos == tiles - 2)
        def _():
            @pl.when(mz > 0)
            def _():
                to_right.wait_recv()

            raw[slot, :, :LANES] = halo[0]

        @pl.when(pos == tiles - 1)
        def _():
            @pl.when(mz < n_mz - 1)
            def _():
                to_left.wait_recv()

            raw[slot, :, tile + LANES :] = halo[1]

        w = w_ref[...]
        done = []
        for j in range(tile // OUT):
            window = raw[slot, :, j * OUT : j * OUT + WIN]
            smooth = jnp.dot(window, w, preferred_element_type=jnp.float32)
            mine = raw[slot, :, LANES + j * OUT : LANES + (j + 1) * OUT].astype(jnp.float32)
            one = (mine - smooth).astype(jnp.bfloat16)
            piece, inside = (j * OUT) // width, (j * OUT) % width
            cleaned[at * per + piece, :, inside : inside + OUT] = one
            done.append(one)
        total[...] += jnp.dot(
            jnp.concatenate(done, axis=1), tap[slot], preferred_element_type=jnp.float32
        )

    @pl.loop(0, tiles)
    def _(pos):
        clean(pos)

        @pl.when(pos + slots < tiles)
        def _():
            each_load(pos + slots, lambda c: c.start())

    @pl.when(mz < n_mz - 1)
    def _():
        to_right.wait_send()

    @pl.when(mz > 0)
    def _():
        to_left.wait_send()

    rows = parts.shape[1]
    for z in range(n_mz):
        parts[z] = total[z * rows : (z + 1) * rows]

    def scatter(d):
        return pltpu.make_async_remote_copy(
            src_ref=parts.at[lax.rem(mz + d, n_mz)], dst_ref=parts_in.at[d - 1],
            send_sem=parts_send.at[d - 1], recv_sem=parts_recv.at[d - 1],
            device_id=at_z(d), device_id_type=MESH,
        )

    for d in range(1, n_mz):
        scatter(d).start()
    mine = parts[mz]
    for d in range(1, n_mz):
        scatter(d).wait_recv()
        mine = mine + parts_in[d - 1]
    sketch[mz] = mine

    def gather(d, owner):
        return pltpu.make_async_remote_copy(
            src_ref=sketch.at[mz], dst_ref=sketch.at[owner],
            send_sem=all_send.at[d - 1], recv_sem=all_recv.at[d - 1],
            device_id=at_z(d), device_id_type=MESH,
        )

    for d in range(1, n_mz):
        gather(d, mz).start()
    for d in range(1, n_mz):
        gather(d, lax.rem(mz + n_mz - d, n_mz)).wait_recv()
    sk = jnp.concatenate([sketch[z] for z in range(n_mz)], axis=0)

    gram[...] = lax.dot_general(
        sk, sk, (((0,), (0,)), ((), ())), precision=HIGHEST, preferred_element_type=jnp.float32
    )

    def share_gram(d):
        return pltpu.make_async_remote_copy(
            src_ref=gram, dst_ref=gram_in.at[d - 1],
            send_sem=gram_send.at[d - 1], recv_sem=gram_recv.at[d - 1],
            device_id=at_pix(d), device_id_type=MESH,
        )

    for d in range(1, n_pix):
        share_gram(d).start()
    full = gram[...]
    for d in range(1, n_pix):
        share_gram(d).wait_recv()
        full = full + gram_in[d - 1]
    total[...] = full * (1.0 / pixels)
    whiten(total, x_ref)
    x = x_ref[...]
    by_lane = (((1,), (1,)), ((), ()))
    flipped = lax.dot_general(
        x, sk, by_lane, precision=HIGHEST, preferred_element_type=jnp.float32
    ).astype(jnp.bfloat16)
    basis_t = flipped.reshape(n_pix, share, flipped.shape[1])
    for chunk in range(n_pix):
        d = lax.rem(chunk // 2 - chip + chips, chips)
        at = d * share + jnp.where(core == chunk % 2, half, 0)
        lhs[pl.ds(pl.multiple_of(at, share), share), :] = basis_t[chunk]

    def to_core(k):
        return pltpu.make_async_remote_copy(
            src_ref=give.at[lax.rem(k, ring)], dst_ref=core_in.at[k],
            send_sem=give_sem.at[lax.rem(k, ring)], recv_sem=core_sem.at[k],
            device_id=device(chip, other), device_id_type=MESH,
        )

    def to_chip(d, k):
        return pltpu.make_async_remote_copy(
            src_ref=x_give.at[d - 1, k], dst_ref=x_in.at[d - 1, k],
            send_sem=x_send_sem.at[d - 1, k], recv_sem=x_recv_sem.at[d - 1, k],
            device_id=device(chip_of(d), core), device_id_type=MESH,
        )

    def first(k):
        slot = lax.rem(k, ring)

        @pl.when(k >= ring)
        def _():
            to_core(k - ring).wait_send()

        part = jnp.dot(lhs[...], cleaned[k], preferred_element_type=jnp.float32) * factor
        part = part.astype(jnp.bfloat16)
        give[slot] = part[:half]
        to_core(k).start()
        hold[slot] = part[half:]

    def second(k):
        to_core(k).wait_recv()
        slot = lax.rem(k, ring)
        added = hold[slot].astype(jnp.float32) + core_in[k].astype(jnp.float32)
        acc[k] = added[:share]
        for d in range(1, chips):
            x_give[d - 1, k] = added[d * share : (d + 1) * share].astype(jnp.bfloat16)
            to_chip(d, k).start()

    def store(k):
        slot = lax.rem(k, ring)
        return pltpu.make_async_copy(
            out_v.at[slot], out.at[:, pl.ds(pl.multiple_of(k * width, width), width)],
            store_sem.at[slot],
        )

    lag = min(ring - 1, chunks)

    @pl.loop(0, lag)
    def _(k):
        first(k)

    basis[...] = lax.dot_general(
        sk, x, by_lane, precision=HIGHEST, preferred_element_type=jnp.float32
    ).astype(jnp.bfloat16)

    @pl.loop(lag, chunks)
    def _(k):
        first(k)
        second(k - lag)

    @pl.loop(chunks - lag, chunks)
    def _(k):
        second(k)

    @pl.loop(max(chunks - ring, 0), chunks)
    def _(k):
        to_core(k).wait_send()

    for d in range(1, n_mz):
        scatter(d).wait_send()
        gather(d, mz).wait_send()
    for d in range(1, n_pix):
        share_gram(d).wait_send()

    @pl.loop(0, chunks)
    def _(k):
        added = acc[k]
        for d in range(1, chips):
            to_chip(d, k).wait()
            added = added + x_in[d - 1, k].astype(jnp.float32)

        @pl.when(k >= ring)
        def _():
            store(k - ring).wait()

        out_v[lax.rem(k, ring)] = added.astype(jnp.bfloat16)
        store(k).start()

    @pl.loop(max(chunks - ring, 0), chunks)
    def _(k):
        store(k).wait()


def per_device(spectra, kernel, probes):
    rows, bins = spectra.shape
    cols = probes.shape[1]
    n_pix, n_mz = lax.axis_size("pix"), lax.axis_size("mz")
    pixels = rows * n_pix
    factor = 1.0 / math.sqrt(float(pixels))
    taps = kernel.shape[0]
    low = WIN - (LANES - taps // 2) - (taps - 1)
    u = jnp.pad(kernel[::-1].astype(jnp.float32), (low, WIN - low - taps))[None, :]
    share = cols // n_pix
    chips = n_pix // 2
    half = chips * share
    tile = min(4096, bins // 2)
    width = min(2048, tile)
    chunks = bins // width
    slots, ring = 3, 4
    away = max(chips - 1, 1)
    part = rows // n_mz
    bf16, f32 = jnp.bfloat16, jnp.float32
    dma = pltpu.SemaphoreType.DMA
    return pl.pallas_call(
        functools.partial(fused_kernel, n_mz, n_pix, factor, float(pixels)),
        in_specs=[
            pl.BlockSpec(memory_space=pl.ANY),
            pl.BlockSpec(memory_space=pltpu.VMEM),
            pl.BlockSpec(memory_space=pl.ANY),
        ],
        out_specs=[pl.BlockSpec(memory_space=pltpu.VMEM), pl.BlockSpec(memory_space=pl.ANY)],
        out_shape=[
            jax.ShapeDtypeStruct((rows, cols), bf16),
            jax.ShapeDtypeStruct((share, bins), bf16),
        ],
        scratch_shapes=[
            pltpu.VMEM((slots, rows, tile + 2 * LANES), bf16),
            pltpu.VMEM((slots, tile, cols), bf16),
            pltpu.VMEM((WIN, OUT), bf16),
            pltpu.VMEM((2, rows, LANES), bf16),
            pltpu.VMEM((chunks, rows, width), bf16),
            pltpu.VMEM((rows, cols), f32),
            pltpu.VMEM((n_mz, part, cols), f32),
            pltpu.VMEM((n_mz - 1, part, cols), f32),
            pltpu.VMEM((n_mz, part, cols), f32),
            pltpu.VMEM((cols, cols), f32),
            pltpu.VMEM((n_pix - 1, cols, cols), f32),
            pltpu.VMEM((cols, cols), f32),
            pltpu.VMEM((cols, rows), bf16),
            pltpu.VMEM((ring, half, width), bf16),
            pltpu.VMEM((chunks, half, width), bf16),
            pltpu.VMEM((ring, half, width), bf16),
            pltpu.VMEM((away, chunks, share, width), bf16),
            pltpu.VMEM((away, chunks, share, width), bf16),
            pltpu.VMEM((chunks, share, width), f32),
            pltpu.VMEM((ring, share, width), bf16),
            dma((slots,)),
            dma((slots,)),
            dma((2,)),
            dma((2,)),
            dma((n_mz - 1,)),
            dma((n_mz - 1,)),
            dma((n_mz - 1,)),
            dma((n_mz - 1,)),
            dma((n_pix - 1,)),
            dma((n_pix - 1,)),
            dma((ring,)),
            dma((chunks,)),
            dma((away, chunks)),
            dma((away, chunks)),
            dma((ring,)),
        ],
        compiler_params=pltpu.CompilerParams(
            collective_id=0, has_side_effects=True, vmem_limit_bytes=58 * 2**20
        ),
        cost_estimate=pl.CostEstimate(
            flops=2 * rows * bins * (WIN + 2 * cols),
            bytes_accessed=2 * bins * (rows + cols + share),
            transcendentals=0,
        ),
    )(spectra, u, probes)


def solution(mesh):
    in_specs = (P(("groups", "pix"), "mz"), P(), P("mz", None))
    out_specs = (P(("groups", "pix"), None), P(("groups", "pix"), "mz"))
    return jax.shard_map(
        per_device, mesh=mesh, in_specs=in_specs, out_specs=out_specs, check_vma=False
    )
```

time: 252 us -> 154 us (0.61)
  waiting for transfers between devices: 69.2 us -> 0 us
  Pallas kernels: 121 us -> 146 us
  other arithmetic: 24.6 us -> 0.66 us
  between operations: 14.1 us -> 0.64 us
  starting transfers between devices: 6.92 us -> 0 us
  local copies, waits for them, and re-layouts: 12.6 us -> 6.67 us
  matrix products: 2.96 us -> 0 us
    psum x2 -> x0, waiting for transfers between devices: 68.4 us -> none  [the longest x1 36.5 us: per_device(): sketch = lax.psum(partial_sketch, 'mz')]
    pallas_call x2 -> x1, Pallas kernels: 121 us -> 146 us  [per_device(): pl.pallas_call(functools.partial(fused_kernel, n_mz, n_pix, factor, float...]
    another operation x5 -> x0, other arithmetic: 22.9 us -> none  [the longest x3 12.4 us: per_device(): lower = jnp.linalg.cholesky(gram)]
    ppermute x2 -> x0, starting transfers between devices: 6.84 us -> none  [the longest x1 5.56 us: per_device(): halo_l = lax.ppermute(spectra[:, bin_cols - LANES:], 'mz', up)]
    unnamed x8 -> x4, local copies, waits for them, and re-layouts: 11.7 us -> 6.67 us
  transfers between devices with their start and end apart: 4 -> 0, of which waited for: 3 -> 0; matrix products, arithmetic and copies ran while one was open for 0% -> 0% of each run, Pallas kernels for 0% -> 0%
where the time goes in v1:
time: 154 us
  Pallas kernels  146 us (95%)
  local copies, waits for them, and re-layouts  6.67 us (4%)
    pallas_call x1, Pallas kernels, per_device(): pl.pallas_call(functools.partial(fused_kernel, n_mz, n_pix, factor, float...  146 us
    unnamed x4, local copies, waits for them, and re-layouts  6.67 us

profile of v1, /device:TPU:0, one launch (start us, length us, event | category | flops | bytes accessed | tf_op | source)
XLA Modules:
  0.0 153.8 jit_solution(15450538406772598673)
XLA Ops:
  0.6 0.7 reverse
  1.4 0.1 slice
  1.5 0.7 pad_convert_fusion
  2.1 145.8 %shard_map.50 = (bf16[128,128]{1,0:T(8,128)(2,1)}, bf16[32,65536]{1,0:T(8,128)(2,1)}) custom-call(bf16[128,65536]{1,0:T(8,128)(2,1)} %spectra.1, f32[1,512]{1,0:T(1,128)} %bitcast.2, bf16[65536,128]{1,0:T(8,128)(2,1)} %probes.1), custom_call_target="tpu_custom_call" | custom-call | flops 12884901888 | bytes 37748736 | tf_op jit(solution)/shard_map/pallas_call | solution.py:383
  148.0 1.4 copy.7
  149.3 4.5 %copy.8 = bf16[32,65536]{1,0:T(8,128)(2,1)} copy(bf16[32,65536]{1,0:T(8,128)(2,1)} %get-tuple-element.5) | data formatting | bytes 8388608

commit v2 on v1

--- a/solution.py
+++ b/solution.py
@@ -21,37 +21,40 @@
 def whiten(a_ref, x_ref):
     size = a_ref.shape[0]
     row = lax.broadcasted_iota(jnp.int32, (PANEL, 1), 0)
-    x_ref[...] = (
+    a = a_ref[...]
+    x = (
         lax.broadcasted_iota(jnp.int32, (size, size), 0)
         == lax.broadcasted_iota(jnp.int32, (size, size), 1)
     ).astype(jnp.float32)
-
-    def panel(index, carry):
-        a, x = carry
-        p, q = a[:PANEL], x[:PANEL]
+    blocks = size // PANEL
+    a = [a[i * PANEL : (i + 1) * PANEL] for i in range(blocks)]
+    x = [x[i * PANEL : (i + 1) * PANEL] for i in range(blocks)]
+    for index in range(blocks):
+        p, q = a[index], x[index]
         rows_p, rows_q = [], []
+        spread = [
+            jnp.broadcast_to(p[:, index * PANEL + t : index * PANEL + t + 1], p.shape)
+            for t in range(PANEL)
+        ]
         for t in range(PANEL):
-            inv = lax.rsqrt(p[t : t + 1, t : t + 1])
+            inv = lax.rsqrt(spread[t][t : t + 1])
             r, y = p[t : t + 1] * inv, q[t : t + 1] * inv
             rows_p.append(r)
             rows_q.append(y)
             if t + 1 < PANEL:
-                scale = jnp.where(row > t, p[:, t : t + 1] * inv, 0.0)
+                scale = jnp.where(row > t, spread[t] * inv, 0.0)
                 p = p - scale * r
                 q = q - scale * y
-        r, y = jnp.concatenate(rows_p, axis=0), jnp.concatenate(rows_q, axis=0)
-        x_ref[pl.ds(pl.multiple_of(index * PANEL, PANEL), PANEL), :] = y
-        turned = r.T
-        rest_a, rest_x = a[PANEL:], x[PANEL:]
-        for t in range(PANEL):
-            scale = turned[PANEL:, t : t + 1]
-            rest_a = rest_a - scale * r[t : t + 1]
-            rest_x = rest_x - scale * y[t : t + 1]
-        zeros = jnp.zeros((PANEL, size), jnp.float32)
-        rest_a = pltpu.roll(rest_a, size - PANEL, 1)
-        return jnp.concatenate([rest_a, zeros], axis=0), jnp.concatenate([rest_x, zeros], axis=0)
-
-    lax.fori_loop(0, size // PANEL, panel, (a_ref[...], x_ref[...]))
+                for j in range(t + 1, PANEL):
+                    spread[j] = spread[j] - scale * (spread[j][t : t + 1] * inv)
+        x_ref[index * PANEL : (index + 1) * PANEL, :] = jnp.concatenate(rows_q, axis=0)
+        if index + 1 < blocks:
+            turned = jnp.concatenate(rows_p, axis=0).T
+            for later in range(index + 1, blocks):
+                for t in range(PANEL):
+                    scale = turned[later * PANEL : (later + 1) * PANEL, t : t + 1]
+                    a[later] = a[later] - scale * rows_p[t]
+                    x[later] = x[later] - scale * rows_q[t]
 
 
 def fused_kernel(

time: 154 us -> 143 us (0.929)
  Pallas kernels: 146 us -> 135 us
    pallas_call x1, Pallas kernels: 146 us -> 135 us  [per_device(): pl.pallas_call(functools.partial(fused_kernel, n_mz, n_pix, factor, float...]
where the time goes in v2:
time: 143 us
  Pallas kernels  135 us (94%)
  local copies, waits for them, and re-layouts  6.67 us (5%)
    pallas_call x1, Pallas kernels, per_device(): pl.pallas_call(functools.partial(fused_kernel, n_mz, n_pix, factor, float...  135 us
    unnamed x4, local copies, waits for them, and re-layouts  6.67 us

profile of v2, /device:TPU:0, one launch (start us, length us, event | category | flops | bytes accessed | tf_op | source)
XLA Modules:
  0.0 142.7 jit_solution(15691084560216000745)
XLA Ops:
  0.6 0.7 reverse
  1.4 0.1 slice
  1.5 0.7 pad_convert_fusion
  2.1 134.7 %shard_map.50 = (bf16[128,128]{1,0:T(8,128)(2,1)}, bf16[32,65536]{1,0:T(8,128)(2,1)}) custom-call(bf16[128,65536]{1,0:T(8,128)(2,1)} %spectra.1, f32[1,512]{1,0:T(1,128)} %bitcast.2, bf16[65536,128]{1,0:T(8,128)(2,1)} %probes.1), custom_call_target="tpu_custom_call" | custom-call | flops 12884901888 | bytes 37748736 | tf_op jit(solution)/shard_map/pallas_call | solution.py:386
  136.8 1.4 copy.7
  138.2 4.5 %copy.8 = bf16[32,65536]{1,0:T(8,128)(2,1)} copy(bf16[32,65536]{1,0:T(8,128)(2,1)} %get-tuple-element.5) | data formatting | bytes 8388608

commit v3 on v2

--- a/solution.py
+++ b/solution.py
@@ -16,6 +16,8 @@
 MESH = pl.DeviceIdType.MESH
 HIGHEST = lax.Precision.HIGHEST
 PANEL = 8
+EARLY = 3
+AHEAD = 2
 
 
 def whiten(a_ref, x_ref):
@@ -58,11 +60,12 @@
 
 
 def fused_kernel(
-    n_mz, n_pix, factor, pixels, spectra, u_ref, probes, basis, out,
+    n_mz, n_pix, factor, pixels, early, ahead, spectra, u_ref, probes, basis, out,
     raw, tap, w_ref, halo, cleaned, total, parts, parts_in, sketch, gram, gram_in, x_ref,
-    lhs, give, core_in, hold, x_give, x_in, acc, out_v,
+    lhs, give, core_in, hold, x_give, x_in, acc, out_v, lhs_far, early_in, sketch_far,
     raw_sem, tap_sem, halo_send, halo_recv, parts_send, parts_recv, all_send, all_recv,
     gram_send, gram_recv, give_sem, core_sem, x_send_sem, x_recv_sem, store_sem,
+    early_send, early_recv, far_send, far_recv,
 ):
     bins = spectra.shape[1]
     slots, tile = tap.shape[0], tap.shape[1]
@@ -117,6 +120,22 @@
         begin = pl.multiple_of(tile_of(pos) * tile, tile)
         act(pltpu.make_async_copy(probes.at[pl.ds(begin, tile), :], tap.at[slot], tap_sem.at[slot]))
 
+    both = chunks - 2 * early
+
+    def whole_of(e, at_chip):
+        return per + 2 * e + at_chip
+
+    def chunk_of(i):
+        return jnp.where(i < per, i, jnp.where(
+            i < both, i + 2 * early, whole_of(i - both, chip)))
+
+    def send_early(e):
+        return pltpu.make_async_remote_copy(
+            src_ref=cleaned.at[whole_of(e, 1 - chip)], dst_ref=early_in.at[e],
+            send_sem=early_send.at[e], recv_sem=early_recv.at[e],
+            device_id=device(1 - chip, core), device_id_type=MESH,
+        )
+
     for pos in range(min(slots, tiles)):
         each_load(jnp.int32(pos), lambda c: c.start())
 
@@ -202,6 +221,11 @@
         def _():
             each_load(pos + slots, lambda c: c.start())
 
+        if ahead:
+            @pl.when(pos < ahead)
+            def _():
+                send_early(pos).start()
+
     @pl.when(mz < n_mz - 1)
     def _():
         to_right.wait_send()
@@ -255,22 +279,36 @@
 
     for d in range(1, n_pix):
         share_gram(d).start()
+    to_far = pltpu.make_async_remote_copy(
+        src_ref=sketch, dst_ref=sketch_far, send_sem=far_send.at[0], recv_sem=far_recv.at[0],
+        device_id=device(1 - chip, core), device_id_type=MESH,
+    )
+    if early:
+        to_far.start()
     full = gram[...]
     for d in range(1, n_pix):
         share_gram(d).wait_recv()
         full = full + gram_in[d - 1]
+    if early:
+        to_far.wait_recv()
+        for e in range(ahead, early):
+            send_early(e).start()
     total[...] = full * (1.0 / pixels)
     whiten(total, x_ref)
     x = x_ref[...]
     by_lane = (((1,), (1,)), ((), ()))
-    flipped = lax.dot_general(
-        x, sk, by_lane, precision=HIGHEST, preferred_element_type=jnp.float32
-    ).astype(jnp.bfloat16)
-    basis_t = flipped.reshape(n_pix, share, flipped.shape[1])
-    for chunk in range(n_pix):
-        d = lax.rem(chunk // 2 - chip + chips, chips)
-        at = d * share + jnp.where(core == chunk % 2, half, 0)
-        lhs[pl.ds(pl.multiple_of(at, share), share), :] = basis_t[chunk]
+
+    def fill(target, of):
+        flipped = lax.dot_general(
+            x, of, by_lane, precision=HIGHEST, preferred_element_type=jnp.float32
+        ).astype(jnp.bfloat16)
+        basis_t = flipped.reshape(n_pix, share, flipped.shape[1])
+        for chunk in range(n_pix):
+            d = lax.rem(chunk // 2 - chip + chips, chips)
+            at = d * share + jnp.where(core == chunk % 2, half, 0)
+            target[pl.ds(pl.multiple_of(at, share), share), :] = basis_t[chunk]
+
+    fill(lhs, sk)
 
     def to_core(k):
         return pltpu.make_async_remote_copy(
@@ -286,81 +324,117 @@
             device_id=device(chip_of(d), core), device_id_type=MESH,
         )
 
-    def first(k):
-        slot = lax.rem(k, ring)
-
-        @pl.when(k >= ring)
-        def _():
-            to_core(k - ring).wait_send()
-
-        part = jnp.dot(lhs[...], cleaned[k], preferred_element_type=jnp.float32) * factor
-        part = part.astype(jnp.bfloat16)
+    def product(left, right):
+        part = jnp.dot(left, right, preferred_element_type=jnp.float32) * factor
+        return part.astype(jnp.bfloat16)
+
+    def first(i, alone):
+        slot = lax.rem(i, ring)
+
+        @pl.when(i >= ring)
+        def _():
+            to_core(i - ring).wait_send()
+
+        part = product(lhs[...], cleaned[chunk_of(i)])
+        if alone:
+            send_early(i - both).wait_recv()
+            far = product(lhs_far[...], early_in[i - both])
+            part = (part.astype(jnp.float32) + far.astype(jnp.float32)).astype(jnp.bfloat16)
         give[slot] = part[:half]
-        to_core(k).start()
+        to_core(i).start()
         hold[slot] = part[half:]
 
-    def second(k):
-        to_core(k).wait_recv()
-        slot = lax.rem(k, ring)
-        added = hold[slot].astype(jnp.float32) + core_in[k].astype(jnp.float32)
+    def second(i):
+        to_core(i).wait_recv()
+        slot = lax.rem(i, ring)
+        k = chunk_of(i)
+        added = hold[slot].astype(jnp.float32) + core_in[i].astype(jnp.float32)
         acc[k] = added[:share]
         for d in range(1, chips):
             x_give[d - 1, k] = added[d * share : (d + 1) * share].astype(jnp.bfloat16)
             to_chip(d, k).start()
 
-    def store(k):
-        slot = lax.rem(k, ring)
+    def store(n, k):
+        slot = lax.rem(n, ring)
         return pltpu.make_async_copy(
             out_v.at[slot], out.at[:, pl.ds(pl.multiple_of(k * width, width), width)],
             store_sem.at[slot],
         )
 
-    lag = min(ring - 1, chunks)
+    def emit(n, k, value):
+        @pl.when(n >= ring)
+        def _():
+            store(n - ring, k).wait()
+
+        out_v[lax.rem(n, ring)] = value.astype(jnp.bfloat16)
+        store(n, k).start()
+
+    lag = min(ring - 1, both)
+    mine = chunks - early
 
     @pl.loop(0, lag)
-    def _(k):
-        first(k)
+    def _(i):
+        first(i, False)
 
     basis[...] = lax.dot_general(
         sk, x, by_lane, precision=HIGHEST, preferred_element_type=jnp.float32
     ).astype(jnp.bfloat16)
 
-    @pl.loop(lag, chunks)
-    def _(k):
-        first(k)
-        second(k - lag)
-
-    @pl.loop(chunks - lag, chunks)
-    def _(k):
-        second(k)
-
-    @pl.loop(max(chunks - ring, 0), chunks)
-    def _(k):
-        to_core(k).wait_send()
+    @pl.loop(lag, both)
+    def _(i):
+        first(i, False)
+        second(i - lag)
+
+    if early:
+        fill(lhs_far, jnp.concatenate([sketch_far[z] for z in range(n_mz)], axis=0))
+
+        @pl.loop(both, mine)
+        def _(i):
+            first(i, True)
+            second(i - lag)
+
+    @pl.loop(mine - lag, mine)
+    def _(i):
+        second(i)
+
+    @pl.loop(max(mine - ring, 0), mine)
+    def _(i):
+        to_core(i).wait_send()
 
     for d in range(1, n_mz):
         scatter(d).wait_send()
         gather(d, mz).wait_send()
     for d in range(1, n_pix):
         share_gram(d).wait_send()
-
-    @pl.loop(0, chunks)
-    def _(k):
+    if early:
+        to_far.wait_send()
+        for e in range(early):
+            send_early(e).wait_send()
+
+        @pl.loop(0, early)
+        def _(e):
+            emit(e, whole_of(e, chip), acc[whole_of(e, chip)])
+
+    @pl.loop(0, both)
+    def _(i):
+        k = chunk_of(i)
         added = acc[k]
         for d in range(1, chips):
             to_chip(d, k).wait()
             added = added + x_in[d - 1, k].astype(jnp.float32)
-
-        @pl.when(k >= ring)
-        def _():
-            store(k - ring).wait()
-
-        out_v[lax.rem(k, ring)] = added.astype(jnp.bfloat16)
-        store(k).start()
+        emit(early + i, k, added)
+
+    if early:
+        @pl.loop(0, early)
+        def _(e):
+            k = whole_of(e, 1 - chip)
+            to_chip(1, k).wait_recv()
+            emit(early + both + e, k, x_in[0, k])
+            to_chip(1, whole_of(e, chip)).wait_send()
 
     @pl.loop(max(chunks - ring, 0), chunks)
-    def _(k):
-        store(k).wait()
+    def _(n):
+        store(n, n).wait()
 
 
 def per_device(spectra, kernel, probes):
@@ -379,12 +453,15 @@
     width = min(2048, tile)
     chunks = bins // width
     slots, ring = 3, 4
+    fits = chips == 2 and tile == 2 * width and bins // tile >= 8
+    early, ahead = (EARLY, AHEAD) if fits else (0, 0)
+    kept = max(early, 1)
     away = max(chips - 1, 1)
     part = rows // n_mz
     bf16, f32 = jnp.bfloat16, jnp.float32
     dma = pltpu.SemaphoreType.DMA
     return pl.pallas_call(
-        functools.partial(fused_kernel, n_mz, n_pix, factor, float(pixels)),
+        functools.partial(fused_kernel, n_mz, n_pix, factor, float(pixels), early, ahead),
         in_specs=[
             pl.BlockSpec(memory_space=pl.ANY),
             pl.BlockSpec(memory_space=pltpu.VMEM),
@@ -416,6 +493,9 @@
             pltpu.VMEM((away, chunks, share, width), bf16),
             pltpu.VMEM((chunks, share, width), f32),
             pltpu.VMEM((ring, share, width), bf16),
+            pltpu.VMEM((cols, rows), bf16),
+            pltpu.VMEM((kept, rows, width), bf16),
+            pltpu.VMEM((n_mz, part, cols), f32),
             dma((slots,)),
             dma((slots,)),
             dma((2,)),
@@ -431,6 +511,10 @@
             dma((away, chunks)),
             dma((away, chunks)),
             dma((ring,)),
+            dma((kept,)),
+            dma((kept,)),
+            dma((1,)),
+            dma((1,)),
         ],
         compiler_params=pltpu.CompilerParams(
             collective_id=0, has_side_effects=True, vmem_limit_bytes=58 * 2**20

time: 143 us -> 139 us (0.972)
  Pallas kernels: 135 us -> 131 us
    pallas_call x1, Pallas kernels: 135 us -> 131 us  [per_device(): pl.pallas_call(functools.partial(fused_kernel, n_mz, n_pix, factor, float...]
where the time goes in v3:
time: 139 us
  Pallas kernels  131 us (94%)
  local copies, waits for them, and re-layouts  6.67 us (5%)
    pallas_call x1, Pallas kernels, per_device(): pl.pallas_call(functools.partial(fused_kernel, n_mz, n_pix, factor, float...  131 us
    unnamed x4, local copies, waits for them, and re-layouts  6.67 us

profile of v3, /device:TPU:0, one launch (start us, length us, event | category | flops | bytes accessed | tf_op | source)
XLA Modules:
  0.0 139.1 jit_solution(51076138247357888)
XLA Ops:
  0.6 0.7 reverse
  1.4 0.1 slice
  1.5 0.7 pad_convert_fusion
  2.1 131.1 %shard_map.50 = (bf16[128,128]{1,0:T(8,128)(2,1)}, bf16[32,65536]{1,0:T(8,128)(2,1)}) custom-call(bf16[128,65536]{1,0:T(8,128)(2,1)} %spectra.1, f32[1,512]{1,0:T(1,128)} %bitcast.2, bf16[65536,128]{1,0:T(8,128)(2,1)} %probes.1), custom_call_target="tpu_custom_call" | custom-call | flops 12884901888 | bytes 37748736 | tf_op jit(solution)/shard_map/pallas_call | solution.py:463
  133.2 1.4 copy.7
  134.6 4.5 %copy.8 = bf16[32,65536]{1,0:T(8,128)(2,1)} copy(bf16[32,65536]{1,0:T(8,128)(2,1)} %get-tuple-element.5) | data formatting | bytes 8388608
